TPU v7x, 32 devices: a whole 2x2x4 slice. The times are simulated.
32 devices in a mesh: grp: 2 (over x), dev: 16 (over z, y, core).
Axes of the slice: x: 2, y: 2, z: 4, core: 2. Of those that a mesh axis runs over, the one named last changes fastest.
Arguments:
- frames: bfloat16 [80, 64, 1408], P('dev'), may hold values from -100 to 100
- trained: int32 [80], replicated, may hold values from 0 to 3071, as said below
- frame_of: int32 [6144], P('dev'), may hold values from 0 to 3071, as said below
- token_cache: bfloat16 [6144, 1408], P('dev'), may hold values from -100 to 100
- norm_gains: float32 [2, 1408], P('grp'), may hold values from 0.1 to 1.9
- proj_weights: bfloat16 [2, 1408, 4224], P('grp'), may hold values from -4 to 4
- out_weights: bfloat16 [2, 1408, 1408], P('grp'), may hold values from -0.15625 to 0.15625
- patch_cotangent: bfloat16 [80, 64, 1408], P('dev'), may hold values from -0.119628906 to 0.119628906
- time_cotangent: bfloat16 [6144, 1408], P('dev'), may hold values from -6 to 6
Outputs:
- weight_grad: float32 [2, 1408, 1408], P('grp', 'dev')
Inputs may be any that keep to these rules, and one draw needn't show every extreme that they name: `trained`: 80 different frames of the video; among them, for every k, the frames k * 192 and (k + 1) * 192 - 1. `frame_of`: never falls along the tokens; tokens 4 m to 4 m + 3 belong to frames 2 m and 2 m + 1, each frame having 1 to 3 tokens.
All inputs are finite; a program needn't handle non-finite values.
Results may differ from a plain program's by a relative error of at most 0.0078.
Values may be sent and summed in bfloat16 or wider, within the bound.
A program may use at most 192 MiB of HBM per device.

v0:
```python
import functools

import jax
import jax.numpy as jnp
from jax import lax
from jax.experimental import pallas as pl
from jax.experimental.pallas import tpu as pltpu
from jax.sharding import PartitionSpec as P

HEADS = 16
HEAD_DIM = 88
SPAN = 128


EPS = 1e-06
HIGH_PRECISION = lax.Precision.HIGHEST


def neighbours(array, rows):
    count = lax.axis_size("dev")
    length = array.shape[0]
    up = [(count + i, count + i + 1) for i in range(count - 1)]
    down = [(target, source) for source, target in up]
    before = lax.ppermute(array[length - rows :], ("grp", "dev"), up)
    after = lax.ppermute(array[:rows], ("grp", "dev"), down)
    return jnp.concatenate([before, array, after], axis=0)


def normalize(rows):
    inverse = lax.rsqrt(jnp.mean(rows * rows, axis=-1, keepdims=True) + EPS)
    return (rows * inverse, inverse)


def when_true(flag, compute):

    def skipped():
        return jax.tree.map(jnp.zeros_like, compute())

    return lax.cond(flag, compute, skipped)


def contract_rows(left, right):
    return lax.dot_general(
        left, right, (((0,), (0,)), ((), ())), preferred_element_type=jnp.float32
    )


def contract_exact(left, right):
    return lax.dot_general(left, right, (((0,), (0,)), ((), ())), precision=HIGH_PRECISION)


def halves(value):
    high = lax.reduce_precision(value, 8, 7)
    return high.astype(jnp.bfloat16), (value - high).astype(jnp.bfloat16)


def lined(rows, lines):
    flat = rows.reshape(rows.shape[0], -1)
    return jnp.pad(flat, ((0, 0), (0, lines * 128 - flat.shape[1]))).reshape(-1, lines, 128)


def unlined(lines, count, width):
    flat = lines.reshape(lines.shape[0], -1)[:, : count * width]
    return flat.reshape(lines.shape[0] * count, width)


MESH = pl.DeviceIdType.MESH


def spread_kernel(count, own, out, send_sem, recv_sem):
    group = lax.axis_index("grp")
    me = lax.axis_index("dev")
    barrier = pltpu.get_barrier_semaphore()

    def copy(slot, target, group_to):
        return pltpu.make_async_remote_copy(
            src_ref=own,
            dst_ref=out.at[slot],
            send_sem=send_sem.at[target],
            recv_sem=recv_sem.at[slot],
            device_id=(group_to, target),
            device_id_type=MESH,
        )

    @pl.when(group == 1)
    def _():
        @pl.loop(0, count)
        def _(j):
            pl.semaphore_signal(barrier, inc=1, device_id=(0, j), device_id_type=MESH)

    @pl.when(group == 0)
    def _():
        pl.semaphore_wait(barrier, count)

        @pl.loop(0, count)
        def _(j):
            copy(me, lax.rem(me + j, count), 1).start()

        @pl.loop(0, count)
        def _(j):
            copy(me, lax.rem(me + j, count), 1).wait_send()

    @pl.when(group == 1)
    def _():
        @pl.loop(0, count)
        def _(j):
            copy(j, j, 0).wait_recv()


def spread(own, count):
    return pl.pallas_call(
        functools.partial(spread_kernel, count),
        out_shape=jax.ShapeDtypeStruct((count,) + own.shape, own.dtype),
        in_specs=[pl.BlockSpec(memory_space=pltpu.VMEM)],
        out_specs=pl.BlockSpec(memory_space=pltpu.VMEM),
        scratch_shapes=[pltpu.SemaphoreType.DMA((count,)), pltpu.SemaphoreType.DMA((count,))],
        compiler_params=pltpu.CompilerParams(
            collective_id=1, has_side_effects=True, vmem_limit_bytes=32 << 20
        ),
    )(own)


def collect_kernel(
    count, parts, sums, grads_out, sums_out, landed, part_send, part_recv, sum_send, sum_recv,
    grad_send, grad_recv,
):
    group = lax.axis_index("grp")
    me = lax.axis_index("dev")
    barrier = pltpu.get_barrier_semaphore()

    def part_copy(slot, target, group_to):
        return pltpu.make_async_remote_copy(
            src_ref=parts.at[target],
            dst_ref=landed.at[slot],
            send_sem=part_send.at[target],
            recv_sem=part_recv.at[slot],
            device_id=(group_to, target),
            device_id_type=MESH,
        )

    def sum_copy(slot, target):
        return pltpu.make_async_remote_copy(
            src_ref=sums,
            dst_ref=sums_out.at[slot],
            send_sem=sum_send.at[target],
            recv_sem=sum_recv.at[slot],
            device_id=(0, target),
            device_id_type=MESH,
        )

    def grad_copy(slot, target):
        return pltpu.make_async_remote_copy(
            src_ref=grads_out.at[me],
            dst_ref=grads_out.at[slot],
            send_sem=grad_send.at[target],
            recv_sem=grad_recv.at[slot],
            device_id=(0, target),
            device_id_type=MESH,
        )

    @pl.when(group == 0)
    def _():
        @pl.loop(0, count)
        def _(j):
            pl.semaphore_signal(barrier, inc=1, device_id=(1, j), device_id_type=MESH)

        @pl.loop(1, count)
        def _(j):
            pl.semaphore_signal(
                barrier, inc=1, device_id=(0, lax.rem(me + j, count)), device_id_type=MESH
            )

        pl.semaphore_wait(barrier, count - 1)

        @pl.loop(1, count)
        def _(j):
            sum_copy(me, lax.rem(me + j, count)).start()

        sums_out[me] = sums[...]

        @pl.loop(1, count)
        def _(j):
            other = lax.rem(me + j, count)
            sum_copy(other, other).wait_recv()

        @pl.loop(1, count)
        def _(j):
            sum_copy(me, lax.rem(me + j, count)).wait_send()

    @pl.when(group == 1)
    def _():
        pl.semaphore_wait(barrier, count)

        @pl.loop(0, count)
        def _(j):
            part_copy(me, lax.rem(me + j, count), 0).start()

        @pl.loop(0, count)
        def _(j):
            part_copy(me, lax.rem(me + j, count), 0).wait_send()

    @pl.when(group == 0)
    def _():
        @pl.loop(0, count)
        def _(j):
            part_copy(j, j, 1).wait_recv()

        total = jnp.sum(landed[...].astype(jnp.float32), axis=0)
        grads_out[me] = total.astype(jnp.bfloat16)

        @pl.loop(1, count)
        def _(j):
            grad_copy(me, lax.rem(me + j, count)).start()

        @pl.loop(1, count)
        def _(j):
            other = lax.rem(me + j, count)
            grad_copy(other, other).wait_recv()

        @pl.loop(1, count)
        def _(j):
            grad_copy(me, lax.rem(me + j, count)).wait_send()


def collect(parts, sums, count):
    vmem = pl.BlockSpec(memory_space=pltpu.VMEM)
    return pl.pallas_call(
        functools.partial(collect_kernel, count),
        out_shape=(
            jax.ShapeDtypeStruct(parts.shape, parts.dtype),
            jax.ShapeDtypeStruct((count,) + sums.shape, sums.dtype),
        ),
        in_specs=[vmem, vmem],
        out_specs=(vmem, vmem),
        scratch_shapes=[pltpu.VMEM(parts.shape, parts.dtype)]
        + [pltpu.SemaphoreType.DMA((count,)) for _ in range(6)],
        compiler_params=pltpu.CompilerParams(
            collective_id=2, has_side_effects=True, vmem_limit_bytes=32 << 20
        ),
    )(parts, sums)


def contract_cols(left, right):
    return lax.dot_general(
        left, right, (((1,), (1,)), ((), ())), preferred_element_type=jnp.float32
    )


def dot_cols(left, right):
    return lax.dot_general(
        left, right, (((1,), (1,)), ((), ())), preferred_element_type=jnp.float32
    )


def dot_rows(left, right):
    return lax.dot_general(
        left, right, (((0,), (0,)), ((), ())), preferred_element_type=jnp.float32
    )


def dot_plain(left, right):
    return jnp.dot(left, right, preferred_element_type=jnp.float32)


SCALE = HEAD_DIM ** (-0.5)
WINDOW = 256


def block(index, count=1):
    return slice(index * SPAN, (index + count) * SPAN)


def head_window(head, width):
    first = head * HEAD_DIM
    start = pl.multiple_of(jnp.minimum(first // 128, (width - WINDOW) // 128) * 128, 128)
    lane = lax.broadcasted_iota(jnp.int32, (1, WINDOW), 1) + start
    return start, (lane >= first) & (lane < first + HEAD_DIM)


def blend(ref, rows, columns, mask, value):
    old = ref[rows, columns].astype(jnp.float32)
    ref[rows, columns] = jnp.where(mask, value, old).astype(ref.dtype)


def attend_kernel(packed, grad, bias, mixed, log_total, row_delta):
    width = grad.shape[1]
    blocks = grad.shape[0] // SPAN
    lanes = lax.broadcasted_iota(jnp.int32, (1, 128), 1)

    def one_head(head, carry):
        start, mask = head_window(head, width)
        keep = mask.astype(jnp.float32).astype(jnp.bfloat16)
        here = pl.ds(start, WINDOW)
        key_at = pl.ds(pl.multiple_of(start + width, 128), WINDOW)
        value_at = pl.ds(pl.multiple_of(start + 2 * width, 128), WINDOW)
        for i in range(blocks):
            query = packed[block(i + 1), here] * keep
            logits = dot_cols(query, packed[block(i, 3), key_at]) * SCALE + bias[:, block(i, 3)]
            top = jnp.max(logits, axis=-1, keepdims=True)
            raised = jnp.exp(logits - top)
            total = jnp.sum(raised, axis=-1, keepdims=True)
            chances = (raised / total).astype(jnp.bfloat16)
            value = dot_plain(chances, packed[block(i, 3), value_at])
            rounded = value.astype(jnp.bfloat16).astype(jnp.float32)
            product = grad[block(i), here].astype(jnp.float32) * rounded
            delta = jnp.sum(jnp.where(mask, product, 0.0), axis=-1, keepdims=True)
            own = lanes == head
            every = slice(0, 128)
            blend(log_total, block(i), every, own, top + jnp.log(total))
            blend(row_delta, block(i), every, own, delta)
            if 1 <= i < blocks - 1:
                blend(mixed, block(i - 1), here, mask, value)
        return carry

    lax.fori_loop(0, HEADS, one_head, 0, unroll=2)


def grads_kernel(packed, grad, bias, log_total, row_delta, out):
    width = grad.shape[1]
    blocks = grad.shape[0] // SPAN
    lanes = lax.broadcasted_iota(jnp.int32, (1, 128), 1)

    def one_head(head, carry):
        start, mask = head_window(head, width)
        keep = mask.astype(jnp.float32).astype(jnp.bfloat16)
        here = pl.ds(start, WINDOW)
        key_at = pl.ds(pl.multiple_of(start + width, 128), WINDOW)
        value_at = pl.ds(pl.multiple_of(start + 2 * width, 128), WINDOW)
        own = lanes == head
        query = packed[block(1, blocks), here] * keep
        cotangent = grad[:, here] * keep
        chance_of, grad_of = {}, {}
        for i in range(blocks):
            first, span = max(i - 1, 1), 3
            if i == 0:
                first, span = 1, 1
            elif i == blocks - 1:
                first, span = blocks - 2, 1
            else:
                first = i - 1
            at = block(first + 1, span)
            inside = bias[:, at] if span == 3 else bias[:, block(i + 1)]
            total = jnp.sum(jnp.where(own, log_total[block(i), :], 0.0), axis=-1, keepdims=True)
            delta = jnp.sum(jnp.where(own, row_delta[block(i), :], 0.0), axis=-1, keepdims=True)
            keys = packed[at, key_at]
            logits = dot_cols(query[block(i)], keys) * SCALE + inside
            chances = jnp.exp(logits - total)
            slope = dot_cols(cotangent[block(i)], packed[at, value_at])
            logit_grad = (chances * (slope - delta)).astype(jnp.bfloat16)
            chances = chances.astype(jnp.bfloat16)
            for step in range(span):
                chance_of[i, first + step] = chances[:, block(step)]
                grad_of[i, first + step] = logit_grad[:, block(step)]
            if span == 3:
                blend(out, block(i - 1), here, mask, dot_plain(logit_grad, keys) * SCALE)
        for j in range(1, blocks - 1):
            rows = block(j - 1, 3)
            near = range(j - 1, j + 2)
            scores = jnp.concatenate([grad_of[i, j] for i in near], axis=0)
            blend(out, block(j - 1), key_at, mask, dot_rows(scores, query[rows]) * SCALE)
            weights = jnp.concatenate([chance_of[i, j] for i in near], axis=0)
            blend(out, block(j - 1), value_at, mask, dot_rows(weights, cotangent[rows]))
        return carry

    lax.fori_loop(0, HEADS, one_head, 0, unroll=2)


def local_call(kernel, out_shape, *operands):
    return pl.pallas_call(
        kernel,
        out_shape=out_shape,
        in_specs=[pl.BlockSpec(memory_space=pltpu.VMEM)] * len(operands),
        out_specs=jax.tree.map(lambda _: pl.BlockSpec(memory_space=pltpu.VMEM), out_shape),
        compiler_params=pltpu.CompilerParams(vmem_limit_bytes=48 << 20),
    )(*operands)


def shards(
    frames,
    trained,
    frame_of,
    token_cache,
    norm_gains,
    proj_weights,
    out_weights,
    patch_cotangent,
    time_cotangent,
):
    spatial = lax.axis_index("grp") == 0
    temporal = jnp.logical_not(spatial)
    norm_gain = norm_gains[0]
    in_proj = proj_weights[0]
    out_proj = out_weights[0]
    width = in_proj.shape[0]
    frame_count, patches, _ = frames.shape
    token_count = token_cache.shape[0]
    devices = lax.axis_size("dev")
    lines = -(-frame_count * width // 2048) * 16
    blocks = token_count // SPAN
    near_tokens = neighbours(token_cache, 2 * SPAN)
    near_frames = neighbours(frame_of, 2 * SPAN)
    near_cotangent = neighbours(time_cotangent, SPAN)
    own_rows = slice(2 * SPAN, 2 * SPAN + token_count)
    block_at = lax.axis_index("dev") * blocks - 2 + jnp.arange((blocks + 4) * SPAN) // SPAN
    bias = jnp.where((block_at >= 0) & (block_at < devices * blocks), 0.0, -1e30)[None, :]

    def spatial_forward():
        rows = frames.reshape(frame_count * patches, width).astype(jnp.float32)
        scaled_rows, _ = normalize(rows)
        normed = (scaled_rows * norm_gain).astype(jnp.bfloat16)
        packed = jnp.dot(normed, in_proj, preferred_element_type=jnp.float32).astype(jnp.bfloat16)
        packed = packed.reshape(frame_count, patches, 3, HEADS, HEAD_DIM)
        attention_logits = (
            jnp.einsum(
                "fphd,fqhd->fhpq",
                packed[:, :, 0],
                packed[:, :, 1],
                preferred_element_type=jnp.float32,
            )
            * SCALE
        )
        attention_probs = jax.nn.softmax(attention_logits, axis=-1).astype(jnp.bfloat16)
        attended_output = jnp.einsum(
            "fhpq,fqhd->fphd", attention_probs, packed[:, :, 2], preferred_element_type=jnp.float32
        )
        attended_output = attended_output.astype(jnp.bfloat16).reshape(frame_count * patches, width)
        sums = jnp.sum(
            attended_output.reshape(frame_count, patches, width).astype(jnp.float32), axis=1
        )
        both = jnp.dot(
            jnp.concatenate(halves(sums), axis=0), out_proj, preferred_element_type=jnp.float32
        )
        carried = jnp.mean(rows.reshape(frame_count, patches, width), axis=1)
        pooled = carried + (both[:frame_count] + both[frame_count:]) / patches
        pooled = lined(pooled.astype(jnp.bfloat16).reshape(1, frame_count * width), lines)[0]
        return (pooled, attended_output, sums)

    pooled, spatial_mixed, sums = when_true(spatial, spatial_forward)
    grad_mixed = when_true(
        temporal, lambda: contract_cols(near_cotangent, out_proj).astype(jnp.bfloat16)
    )
    arrived = unlined(spread(pooled, devices), frame_count, width)

    def temporal_forward():
        selector = (near_frames[:, None] == trained[None, :]).astype(jnp.bfloat16)
        inputs = near_tokens.astype(jnp.float32) + jnp.dot(
            selector, arrived, preferred_element_type=jnp.float32
        )
        scaled_rows, inverse = normalize(inputs)
        normed = (scaled_rows * norm_gain).astype(jnp.bfloat16)
        packed = jnp.dot(normed, in_proj, preferred_element_type=jnp.float32).astype(jnp.bfloat16)
        stat = jax.ShapeDtypeStruct(((blocks + 2) * SPAN, 128), jnp.float32)
        time_mixed, log_total, row_delta = local_call(
            attend_kernel,
            (jax.ShapeDtypeStruct((token_count, width), jnp.bfloat16), stat, stat),
            packed, grad_mixed, bias,
        )
        part = contract_rows(time_mixed, time_cotangent).astype(jnp.bfloat16)
        return (
            part, packed, log_total, row_delta,
            selector[own_rows], scaled_rows[own_rows], inverse[own_rows],
        )

    def from_frames():
        part = contract_rows(
            spatial_mixed, patch_cotangent.reshape(frame_count * patches, width)
        ).astype(jnp.bfloat16)
        skipped = jax.tree.map(
            lambda leaf: jnp.zeros(leaf.shape, leaf.dtype), jax.eval_shape(temporal_forward)[1:]
        )
        return (part,) + tuple(skipped)

    part, packed, log_total, row_delta, selector, scaled_rows, inverse = lax.cond(
        spatial, from_frames, temporal_forward
    )
    weight_part = lax.psum_scatter(part, "dev", scatter_dimension=0, tiled=True).astype(jnp.float32)

    def temporal_back():
        grad_packed = local_call(
            grads_kernel,
            jax.ShapeDtypeStruct((token_count, 3 * width), jnp.bfloat16),
            packed, grad_mixed, bias, log_total, row_delta,
        )
        grad_scaled = contract_cols(grad_packed, in_proj) * norm_gain
        grad_inputs = inverse * (
            grad_scaled - scaled_rows * jnp.mean(grad_scaled * scaled_rows, axis=-1, keepdims=True)
        ) + time_cotangent.astype(jnp.float32)
        high, low = halves(grad_inputs)
        grads = contract_rows(selector, high) + contract_rows(selector, low)
        return lined(grads.astype(jnp.bfloat16).reshape(devices, frame_count * width), lines)

    parts = when_true(temporal, temporal_back)
    grad_lines, sum_lines = collect(
        parts, lined(sums.reshape(1, frame_count * width), lines)[0], devices
    )

    def from_pooled():
        frame_grads = unlined(grad_lines, frame_count, width).astype(jnp.float32)
        all_sums = unlined(sum_lines, frame_count, width)
        share = width // devices
        own_sums = lax.dynamic_slice_in_dim(
            all_sums, lax.axis_index("dev") * share, share, axis=1
        )
        return weight_part + contract_exact(own_sums, frame_grads) / patches

    return lax.cond(spatial, from_pooled, lambda: weight_part)[None]


def solution(mesh):
    in_specs = (
        P("dev", None, None),
        P(),
        P("dev"),
        P("dev", None),
        P("grp", None),
        P("grp", None, None),
        P("grp", None, None),
        P("dev", None, None),
        P("dev", None),
    )
    out_specs = P("grp", "dev", None)
    return jax.shard_map(shards, mesh=mesh, in_specs=in_specs, out_specs=out_specs, check_vma=False)
```

profile of v0, /device:TPU:0, one launch (start us, length us, event | category | flops | bytes accessed | tf_op | source)
XLA Modules:
  0.0 241.1 jit_solution(5010739668017321257)
XLA Ops:
  6.5 0.0 reduce-scatter.4.cloned.1.call-start
  6.6 2.2 fusion.34
  8.7 1.4 collective-permute-start.4
  10.1 1.4 collective-permute-start.5
  11.5 1.3 fusion.35
  12.8 1.5 collective-permute-start
  14.3 1.5 collective-permute-start.1
  15.8 0.5 fusion.36
  16.4 0.6 collective-permute-start.2
  17.0 0.6 and_select_fusion
  17.6 0.0 collective-permute-done.2
  17.6 1.2 collective-permute-start.3
  18.9 0.0 copy-done.7
  18.9 35.8 %conditional.6 = (bf16[64,128]{1,0:T(8,128)(2,1)S(1)}, bf16[320,1408]{1,0:T(8,128)(2,1)}, f32[64,128]{1,0:T(8,128)S(1)}) conditional(s32[]{:T(128)} %convert_element_type.93, () %tuple.46, (bf16[5,64,1408]{2,1,0:T(8,128)(2,1)S(1)}, f32[1,1408]{1,0:T(1,128)S(1)}, bf16[1408,4224]{1,0:T(8,128)(2,1)}, bf16[1408,1408]{1,0:T(8,128)(2,1)}) %tuple.94), branch_computations={%region_0.1_spmd, %region_1.7_spmd} | conditional | flops 3969696256 | bytes 46026272 | solution.py:39
  18.9 0.3 multiply_reduce_fusion.1
  19.3 0.1 rsqrt.22
  19.4 0.3 fusion.9
  19.6 10.2 %convolution_convert_fusion.1 = bf16[320,4224]{1,0:T(8,128)(2,1)} fusion(bf16[320,1408]{1,0:T(8,128)(2,1)S(1)} %fusion.9, bf16[1408,4224]{1,0:T(8,128)(2,1)} %get-tuple-element.93), kind=kOutput, calls=%fused_computation.10 | convolution fusion | flops 3807682560 | bytes 15499264 | tf_op jit(solution)/shard_map/cond/branch_1_fun/dot_general | solution.py:411
  29.9 9.8 %reshape.138 = bf16[5,64,3,16,88]{4,3,2,1,0:T(8,128)(2,1)} reshape(bf16[320,4224]{1,0:T(8,128)(2,1)} %convolution_convert_fusion.1) | data formatting | bytes 5406720 | tf_op jit(solution)/shard_map/cond/branch_1_fun/reshape | solution.py:412
  39.7 3.0 %fusion.32 = (bf16[5,64,1,16,88]{4,3,2,1,0:T(8,128)(2,1)S(1)}, bf16[5,64,1,16,88]{4,3,2,1,0:T(8,128)(2,1)S(1)}, bf16[5,64,1,16,88]{4,3,2,1,0:T(8,128)(2,1)S(1)}) fusion(bf16[5,64,3,16,88]{4,3,2,1,0:T(8,128)(2,1)} %reshape.138), kind=kLoop, calls=%fused_computation.76 | loop fusion | bytes 5406720 | tf_op jit(solution)/shard_map/cond/branch_1_fun/slice | solution.py:424
  42.8 0.8 fusion.11
  43.6 3.9 %fusion.33 = (f32[5,16,64]{2,1,0:T(8,128)S(1)}, f32[5,16,64,64]{2,3,1,0:T(8,128)S(1)}) fusion(f32[5,16,64,64]{2,3,1,0:T(8,128)S(1)} %fusion.11), kind=kOutput, calls=%fused_computation.77 | output fusion | flops 1310783 | bytes 2641920 | tf_op jit(solution)/shard_map/cond/branch_1_fun/sub | solution.py:422
  47.5 0.9 convert_reduce_fusion
  48.4 0.9 copy.29
  49.3 2.2 reshape.141
  51.5 0.1 reshape.142
  51.6 0.1 reduce_sum.53
  51.8 2.8 %fusion.18 = f32[10,1408]{1,0:T(8,128)S(1)} fusion(bf16[1408,1408]{1,0:T(8,128)(2,1)} %get-tuple-element.94, bf16[5,1408]{1,0:T(8,128)(2,1)S(1)} %get-tuple-element.173, bf16[5,1408]{1,0:T(8,128)(2,1)S(1)} %get-tuple-element.172), kind=kOutput, calls=%fused_computation.36 | convolution fusion | flops 39705600 | bytes 4049408 | tf_op jit(solution)/shard_map/cond/branch_1_fun/dot_general | solution.py:430
  54.6 0.1 pad_reduce_fusion
  54.7 5.5 %shard_map.96 = bf16[16,64,128]{2,1,0:T(8,128)(2,1)S(1)} custom-call(bf16[64,128]{1,0:T(8,128)(2,1)S(1)} %get-tuple-element.137.own), custom_call_target="tpu_custom_call" | custom-call | tf_op jit(solution)/shard_map/pallas_call | solution.py:111
  60.2 0.0 collective-permute-done.3
  60.2 0.7 pad_add_fusion
  60.9 0.0 collective-permute-done.4
  60.9 0.0 collective-permute-done.5
  60.9 2.5 %pad_maximum_fusion.1 = bf16[640,1408]{1,0:T(8,128)(2,1)} fusion(bf16[128,1408]{1,0:T(8,128)(2,1)} %collective-permute-done.5, bf16[384,1408]{1,0:T(8,128)(2,1)S(1)} %copy-done.3, bf16[128,1408]{1,0:T(8,128)(2,1)} %collective-permute-done.4), kind=kLoop, calls=%fused_computation.68 | loop fusion | flops 5406720 | bytes 3604480 | tf_op jit(solution)/shard_map/concatenate | solution.py:26
  63.4 0.3 conditional.7
  63.4 0.1 broadcast.181
  63.7 0.0 copy-start
  63.7 0.0 copy-start.8
  63.7 0.0 collective-permute-done
  63.7 0.0 collective-permute-done.1
  63.7 4.0 %pad_maximum_fusion = bf16[896,1408]{1,0:T(8,128)(2,1)} fusion(bf16[256,1408]{1,0:T(8,128)(2,1)} %collective-permute-done.1, bf16[384,1408]{1,0:T(8,128)(2,1)} %param.22, bf16[256,1408]{1,0:T(8,128)(2,1)} %collective-permute-done), kind=kLoop, calls=%fused_computation.67 | loop fusion | flops 7569408 | bytes 5046272 | tf_op jit(solution)/shard_map/concatenate | solution.py:26
  67.8 0.0 copy-done.8
  67.8 0.0 copy-done
  67.8 11.9 %conditional.8 = (bf16[1408,1408]{1,0:T(8,128)(2,1)}, bf16[896,4224]{1,0:T(8,128)(2,1)}, f32[640,128]{1,0:T(8,128)}, f32[640,128]{1,0:T(8,128)}, bf16[384,80]{1,...) conditional(s32[]{:T(128)} %convert_element_type.93, (bf16[896,1408]{1,0:T(8,128)(2,1)}, ...), branch_computations={%region_9.11_spmd, %region_11.12_spmd} | conditional | flops 12394900480 | bytes 68903160
  68.0 5.8 %fusion.37 = bf16[1408,1408]{1,0:T(8,128)(2,1)} fusion(bf16[320,1408]{1,0:T(8,128)(2,1)} %get-tuple-element.109, bf16[320,1408]{1,0:T(8,128)(2,1)} %bitcast.85), kind=kOutput, calls=%fused_computation.81 | convolution fusion | flops 1268776960 | bytes 5767168 | tf_op jit(solution)/shard_map/cond/branch_1_fun/dot_general | solution.py:43
  73.9 0.6 broadcast.186
  74.5 0.7 broadcast.185.clone
  75.2 0.7 broadcast.185
  76.0 0.1 broadcast.187
  76.1 3.5 %broadcast.184 = bf16[896,4224]{1,0:T(8,128)(2,1)} broadcast(bf16[]{:T(256)} %constant.63.clone), dimensions={} | broadcast | bytes 7569410 | tf_op jit(solution)/shard_map/broadcast.31
  79.7 0.0 reduce-scatter.4.cloned.1.call-update
  79.7 0.1 conditional.9
  79.8 113.8 %shard_map.97 = (bf16[16,64,128]{2,1,0:T(8,128)(2,1)S(1)}, f32[16,64,128]{2,1,0:T(8,128)S(1)}) custom-call(bf16[16,64,128]{2,1,0:T(8,128)(2,1)S(1)} %get-tuple-element.214.parts, f32[64,128]{1,0:T(8,128)S(1)} %get-tuple-element.146.sums), custom_call_target="tpu_custom_call" | custom-call | tf_op jit(solution)/shard_map/pallas_call | solution.py:227
  193.6 37.4 %reduce-scatter.4.cloned.1.call-done = bf16[88,1408]{1,0:T(8,128)(2,1)} async-done(((bf16[1408,1408]{1,0:T(8,128)(2,1)}), bf16[88,1408]{1,0:T(8,128)(2,1)}) %reduce-scatter.4.cloned.1.call-update) | async-done | bytes 247824
  231.0 1.0 convert_element_type.96
  232.0 1.5 conditional.20
  232.0 0.3 copy.51
  232.4 0.1 reshape.149
  232.5 0.2 copy.52
  232.7 0.2 reshape.151
  232.9 0.6 fusion.1
  233.5 0.0 copy-start.6
  233.5 0.8 copy-done.6
  (23 shorter events, 0.2 us)
Async XLA Ops:
  6.5 5.0 %copy-start.4 = (bf16[384,1408]{1,0:T(8,128)(2,1)S(1)}, bf16[384,1408]{1,0:T(8,128)(2,1)}, u32[]{:S(2)}) copy-start(bf16[384,1408]{1,0:T(8,128)(2,1)} %param.22) | copy-start | bytes 3244036
  6.5 9.3 %copy-start.10 = (s32[384]{0:T(512)S(1)}, s32[384]{0:T(512)}, u32[]{:S(2)}) copy-start(s32[384]{0:T(512)} %param.21) | copy-start | bytes 4612
  6.5 12.3 %copy-start.7 = (f32[1,1408]{1,0:T(1,128)S(1)}, f32[1,1408]{1,0:T(1,128)}, u32[]{:S(2)}) copy-start(f32[1,1408]{1,0:T(1,128)} %param.23) | copy-start | bytes 16900
  6.5 12.3 %copy-start.5 = (bf16[5,64,1408]{2,1,0:T(8,128)(2,1)S(1)}, bf16[5,64,1408]{2,1,0:T(8,128)(2,1)}, u32[]{:S(2)}) copy-start(bf16[5,64,1408]{2,1,0:T(8,128)(2,1)} %param.19) | copy-start | bytes 2703364
  6.5 224.5 %reduce-scatter.4.cloned.1.call-start = ((), (), s32[]{:S(2)}) async-start(), calls=%async_computation.1 | async-start | bytes 4212736
  8.7 52.1 %collective-permute-start.4 = (bf16[128,1408]{1,0:T(8,128)(2,1)}, bf16[128,1408]{1,0:T(8,128)(2,1)}, u32[]{:S(2)}, u32[]{:S(2)}) collective-permute-start(bf16[128,1408]{1,0:T(8,128)(2,1)} %get-tuple-element.182), channel_id=1, source_target_pairs={{16,17},{17,18},{18,19},{19,20},{20,21},{21,22},{22,23},{23,24},{2... | collective-permute-start | bytes 1081352 | tf_op jit(solution)/shard_map/ppermute | solution.py:24
  10.1 50.7 %collective-permute-start.5 = (bf16[128,1408]{1,0:T(8,128)(2,1)}, bf16[128,1408]{1,0:T(8,128)(2,1)}, u32[]{:S(2)}, u32[]{:S(2)}) collective-permute-start(bf16[128,1408]{1,0:T(8,128)(2,1)} %get-tuple-element.183), channel_id=1, source_target_pairs={{17,16},{18,17},{19,18},{20,19},{21,20},{22,21},{23,22},{24,23},{2... | collective-permute-start | bytes 1081352 | tf_op jit(solution)/shard_map/ppermute | solution.py:25
  12.8 50.9 %collective-permute-start = (bf16[256,1408]{1,0:T(8,128)(2,1)}, bf16[256,1408]{1,0:T(8,128)(2,1)}, u32[]{:S(2)}, u32[]{:S(2)}) collective-permute-start(bf16[256,1408]{1,0:T(8,128)(2,1)} %get-tuple-element.184), channel_id=1, source_target_pairs={{16,17},{17,18},{18,19},{19,20},{20,21},{21,22},{22,23},{23,24},{2... | collective-permute-start | bytes 2162696 | tf_op jit(solution)/shard_map/ppermute | solution.py:24
  14.3 49.4 %collective-permute-start.1 = (bf16[256,1408]{1,0:T(8,128)(2,1)}, bf16[256,1408]{1,0:T(8,128)(2,1)}, u32[]{:S(2)}, u32[]{:S(2)}) collective-permute-start(bf16[256,1408]{1,0:T(8,128)(2,1)} %get-tuple-element.185), channel_id=1, source_target_pairs={{17,16},{18,17},{19,18},{20,19},{21,20},{22,21},{23,22},{24,23},{2... | collective-permute-start | bytes 2162696 | tf_op jit(solution)/shard_map/ppermute | solution.py:25
  16.4 1.3 collective-permute-start.2
  17.6 1.2 copy-start.12
  17.6 42.5 %collective-permute-start.3 = (s32[256]{0:T(256)}, s32[256]{0:T(256)}, u32[]{:S(2)}, u32[]{:S(2)}) collective-permute-start(s32[256]{0:T(256)} %get-tuple-element.187), channel_id=1, source_target_pairs={{17,16},{18,17},{19,18},{20,19},{21,20},{22,21},{23,22},{24,23},{2... | collective-permute-start | bytes 3080 | tf_op jit(solution)/shard_map/ppermute | solution.py:25
  18.9 42.0 %copy-start.3 = (bf16[384,1408]{1,0:T(8,128)(2,1)S(1)}, bf16[384,1408]{1,0:T(8,128)(2,1)}, u32[]{:S(2)}) copy-start(bf16[384,1408]{1,0:T(8,128)(2,1)} %param.27) | copy-start | bytes 3244036
  63.7 4.1 %copy-start = (bf16[640,1408]{1,0:T(8,128)(2,1)}, bf16[640,1408]{1,0:T(8,128)(2,1)S(1)}, u32[]{:S(2)}) copy-start(bf16[640,1408]{1,0:T(8,128)(2,1)S(1)} %get-tuple-element.213) | copy-start | bytes 5406724
  63.7 4.1 %copy-start.8 = (f32[1,1408]{1,0:T(1,128)S(1)}, f32[1,1408]{1,0:T(1,128)}, u32[]{:S(2)}) copy-start(f32[1,1408]{1,0:T(1,128)} %param.23) | copy-start | bytes 16900
  63.7 4.1 %copy-start.9 = (f32[1,896]{1,0:T(1,128)S(1)}, f32[1,896]{1,0:T(1,128)}, u32[]{:S(2)}) copy-start(f32[1,896]{1,0:T(1,128)} %and_select_fusion) | copy-start | bytes 10756
  233.5 0.8 copy-start.6
Sparse Core Ops, SparseCore 0:
  79.8 151.1 reduce-scatter.3
where the time goes:
time: 242 us; the launch traced here: 241 us
  Pallas kernels  119 us (49%)
  waiting for transfers between devices  37.4 us (15%)
  local copies, waits for them, and re-layouts  28 us (12%)
  matrix products  21.1 us (9%)
  between operations  13.5 us (6%)
  other arithmetic  13.4 us (6%)
  starting transfers between devices  7.74 us (3%)
    pallas_call x1, Pallas kernels, collect(): pl.pallas_call(functools.partial(collect_kernel, count), out_shape=(jax.S...  114 us
    unnamed x2, waiting for transfers between devices  37.4 us
    dot_general x1, matrix products, spatial_forward(): jnp.dot(normed, in_proj, preferred_element_type=jnp.float32)  10.2 us
    reshape x1, local copies, waits for them, and re-layouts, spatial_forward(): packed = packed.reshape(frame_count, patches, 3, HEADS, HEAD_DIM)  9.85 us
    concatenate x3, other arithmetic, neighbours(): return jnp.concatenate([before, array, after], axis=0)  7.2 us
    another operation x8, local copies, waits for them, and re-layouts  5.99 us
    dot_general x1, matrix products, contract_rows(): lax.dot_general(left, right, (((0,), (0,)), ((), ())), preferred_element_...  5.82 us
    pallas_call x1, Pallas kernels, spread(): pl.pallas_call(functools.partial(spread_kernel, count), out_shape=jax.Sha...  5.49 us
  transfers between devices with their start and end apart: 7, of which 1 were waited for; matrix products, arithmetic and copies ran while one was open for 17% of the time, Pallas kernels for 49%

commit v1 on v0

--- a/solution.py
+++ b/solution.py
@@ -16,16 +16,6 @@
 HIGH_PRECISION = lax.Precision.HIGHEST
 
 
-def neighbours(array, rows):
-    count = lax.axis_size("dev")
-    length = array.shape[0]
-    up = [(count + i, count + i + 1) for i in range(count - 1)]
-    down = [(target, source) for source, target in up]
-    before = lax.ppermute(array[length - rows :], ("grp", "dev"), up)
-    after = lax.ppermute(array[:rows], ("grp", "dev"), down)
-    return jnp.concatenate([before, array, after], axis=0)
-
-
 def normalize(rows):
     inverse = lax.rsqrt(jnp.mean(rows * rows, axis=-1, keepdims=True) + EPS)
     return (rows * inverse, inverse)
@@ -67,10 +57,14 @@
 MESH = pl.DeviceIdType.MESH
 
 
-def spread_kernel(count, own, out, send_sem, recv_sem):
+def spread_kernel(
+    count, own, tokens, grads, frames, out, near_tokens, near_grads, near_frames, send_sem,
+    recv_sem, side_send, side_recv,
+):
     group = lax.axis_index("grp")
     me = lax.axis_index("dev")
     barrier = pltpu.get_barrier_semaphore()
+    extended = ((tokens, near_tokens, 2 * SPAN), (grads, near_grads, SPAN), (frames, near_frames, 2))
 
     def copy(slot, target, group_to):
         return pltpu.make_async_remote_copy(
@@ -82,11 +76,39 @@
             device_id_type=MESH,
         )
 
+    def side_copies(upward, target):
+        copies = []
+        for at, (source, near, rows) in enumerate(extended):
+            length = source.shape[0]
+            index = at + 3 * upward
+            copies.append(
+                pltpu.make_async_remote_copy(
+                    src_ref=source.at[pl.ds(length - rows if upward else 0, rows)],
+                    dst_ref=near.at[pl.ds(0 if upward else length + rows, rows)],
+                    send_sem=side_send.at[index],
+                    recv_sem=side_recv.at[index],
+                    device_id=(1, target),
+                    device_id_type=MESH,
+                )
+            )
+        return copies
+
+    not_first, not_last = me > 0, me < count - 1
+    above, below = jnp.minimum(me + 1, count - 1), jnp.maximum(me - 1, 0)
+
     @pl.when(group == 1)
     def _():
         @pl.loop(0, count)
         def _(j):
             pl.semaphore_signal(barrier, inc=1, device_id=(0, j), device_id_type=MESH)
+
+        @pl.when(not_first)
+        def _():
+            pl.semaphore_signal(barrier, inc=1, device_id=(1, below), device_id_type=MESH)
+
+        @pl.when(not_last)
+        def _():
+            pl.semaphore_signal(barrier, inc=1, device_id=(1, above), device_id_type=MESH)
 
     @pl.when(group == 0)
     def _():
@@ -102,22 +124,71 @@
 
     @pl.when(group == 1)
     def _():
+        pl.semaphore_wait(barrier, jnp.where(not_first, 1, 0) + jnp.where(not_last, 1, 0))
+
+        @pl.when(not_last)
+        def _():
+            for side in side_copies(1, above):
+                side.start()
+
+        @pl.when(not_first)
+        def _():
+            for side in side_copies(0, below):
+                side.start()
+
+        for source, near, rows in extended:
+            near[rows : rows + source.shape[0]] = source[...]
+
+        @pl.when(jnp.logical_not(not_first))
+        def _():
+            for source, near, rows in extended:
+                near[:rows] = jnp.zeros((rows,) + near.shape[1:], near.dtype)
+
+        @pl.when(jnp.logical_not(not_last))
+        def _():
+            for source, near, rows in extended:
+                near[rows + source.shape[0] :] = jnp.zeros((rows,) + near.shape[1:], near.dtype)
+
+        @pl.when(not_first)
+        def _():
+            for side in side_copies(1, below):
+                side.wait_recv()
+            for side in side_copies(0, below):
+                side.wait_send()
+
+        @pl.when(not_last)
+        def _():
+            for side in side_copies(0, above):
+                side.wait_recv()
+            for side in side_copies(1, above):
+                side.wait_send()
+
         @pl.loop(0, count)
         def _(j):
             copy(j, j, 0).wait_recv()
 
 
-def spread(own, count):
+def spread(own, tokens, grads, frames, count):
+    vmem = pl.BlockSpec(memory_space=pltpu.VMEM)
+
+    def longer(array, rows):
+        return jax.ShapeDtypeStruct((array.shape[0] + 2 * rows,) + array.shape[1:], array.dtype)
+
     return pl.pallas_call(
         functools.partial(spread_kernel, count),
-        out_shape=jax.ShapeDtypeStruct((count,) + own.shape, own.dtype),
-        in_specs=[pl.BlockSpec(memory_space=pltpu.VMEM)],
-        out_specs=pl.BlockSpec(memory_space=pltpu.VMEM),
-        scratch_shapes=[pltpu.SemaphoreType.DMA((count,)), pltpu.SemaphoreType.DMA((count,))],
+        out_shape=(
+            jax.ShapeDtypeStruct((count,) + own.shape, own.dtype),
+            longer(tokens, 2 * SPAN),
+            longer(grads, SPAN),
+            longer(frames, 2),
+        ),
+        in_specs=[vmem] * 4,
+        out_specs=(vmem,) * 4,
+        scratch_shapes=[pltpu.SemaphoreType.DMA((n,)) for n in (count, count, 6, 6)],
         compiler_params=pltpu.CompilerParams(
             collective_id=1, has_side_effects=True, vmem_limit_bytes=32 << 20
         ),
-    )(own)
+    )(own, tokens, grads, frames)
 
 
 def collect_kernel(
@@ -295,18 +366,18 @@
         value_at = pl.ds(pl.multiple_of(start + 2 * width, 128), WINDOW)
         for i in range(blocks):
             query = packed[block(i + 1), here] * keep
-            logits = dot_cols(query, packed[block(i, 3), key_at]) * SCALE + bias[:, block(i, 3)]
+            logits = dot_cols(query, packed[block(i, 3), key_at]) + bias[:, block(i, 3)]
             top = jnp.max(logits, axis=-1, keepdims=True)
-            raised = jnp.exp(logits - top)
+            raised = jnp.exp((logits - top) * SCALE)
             total = jnp.sum(raised, axis=-1, keepdims=True)
-            chances = (raised / total).astype(jnp.bfloat16)
+            chances = (raised * (1.0 / total)).astype(jnp.bfloat16)
             value = dot_plain(chances, packed[block(i, 3), value_at])
             rounded = value.astype(jnp.bfloat16).astype(jnp.float32)
             product = grad[block(i), here].astype(jnp.float32) * rounded
             delta = jnp.sum(jnp.where(mask, product, 0.0), axis=-1, keepdims=True)
             own = lanes == head
             every = slice(0, 128)
-            blend(log_total, block(i), every, own, top + jnp.log(total))
+            blend(log_total, block(i), every, own, top * SCALE + jnp.log(total))
             blend(row_delta, block(i), every, own, delta)
             if 1 <= i < blocks - 1:
                 blend(mixed, block(i - 1), here, mask, value)
@@ -331,13 +402,12 @@
         cotangent = grad[:, here] * keep
         chance_of, grad_of = {}, {}
         for i in range(blocks):
-            first, span = max(i - 1, 1), 3
             if i == 0:
                 first, span = 1, 1
             elif i == blocks - 1:
                 first, span = blocks - 2, 1
             else:
-                first = i - 1
+                first, span = i - 1, 3
             at = block(first + 1, span)
             inside = bias[:, at] if span == 3 else bias[:, block(i + 1)]
             total = jnp.sum(jnp.where(own, log_total[block(i), :], 0.0), axis=-1, keepdims=True)
@@ -397,9 +467,6 @@
     devices = lax.axis_size("dev")
     lines = -(-frame_count * width // 2048) * 16
     blocks = token_count // SPAN
-    near_tokens = neighbours(token_cache, 2 * SPAN)
-    near_frames = neighbours(frame_of, 2 * SPAN)
-    near_cotangent = neighbours(time_cotangent, SPAN)
     own_rows = slice(2 * SPAN, 2 * SPAN + token_count)
     block_at = lax.axis_index("dev") * blocks - 2 + jnp.arange((blocks + 4) * SPAN) // SPAN
     bias = jnp.where((block_at >= 0) & (block_at < devices * blocks), 0.0, -1e30)[None, :]
@@ -433,13 +500,24 @@
         carried = jnp.mean(rows.reshape(frame_count, patches, width), axis=1)
         pooled = carried + (both[:frame_count] + both[frame_count:]) / patches
         pooled = lined(pooled.astype(jnp.bfloat16).reshape(1, frame_count * width), lines)[0]
-        return (pooled, attended_output, sums)
-
-    pooled, spatial_mixed, sums = when_true(spatial, spatial_forward)
-    grad_mixed = when_true(
-        temporal, lambda: contract_cols(near_cotangent, out_proj).astype(jnp.bfloat16)
-    )
-    arrived = unlined(spread(pooled, devices), frame_count, width)
+        grad_mixed = jnp.zeros((token_count, width), jnp.bfloat16)
+        return (pooled, attended_output, sums, grad_mixed)
+
+    def ahead():
+        return (
+            jnp.zeros((lines, 128), jnp.bfloat16),
+            jnp.zeros((frame_count * patches, width), jnp.bfloat16),
+            jnp.zeros((frame_count, width), jnp.float32),
+            contract_cols(time_cotangent, out_proj).astype(jnp.bfloat16),
+        )
+
+    pooled, spatial_mixed, sums, own_grad = lax.cond(spatial, spatial_forward, ahead)
+    frame_lines = jnp.broadcast_to(frame_of.reshape(blocks, 1, SPAN), (blocks, 8, SPAN))
+    arrived, near_tokens, grad_mixed, near_lines = spread(
+        pooled, token_cache, own_grad, frame_lines, devices
+    )
+    arrived = unlined(arrived, frame_count, width)
+    near_frames = near_lines[:, 0].reshape(-1)
 
     def temporal_forward():
         selector = (near_frames[:, None] == trained[None, :]).astype(jnp.bfloat16)
@@ -473,7 +551,19 @@
     part, packed, log_total, row_delta, selector, scaled_rows, inverse = lax.cond(
         spatial, from_frames, temporal_forward
     )
-    weight_part = lax.psum_scatter(part, "dev", scatter_dimension=0, tiled=True).astype(jnp.float32)
+    core = lax.rem(lax.axis_index("dev"), 2)
+    part = part.reshape(devices // 2, 2, width // devices, width)
+    kept = lax.dynamic_index_in_dim(part, core, axis=1, keepdims=False)
+    given = lax.dynamic_index_in_dim(part, 1 - core, axis=1, keepdims=False)
+    taken = lax.ppermute(given, "dev", [(i, i ^ 1) for i in range(devices)])
+    pair = (kept.astype(jnp.float32) + taken.astype(jnp.float32)).astype(jnp.bfloat16)
+    weight_part = lax.psum_scatter(
+        pair.reshape(width // 2, width),
+        "dev",
+        scatter_dimension=0,
+        axis_index_groups=[list(range(start, devices, 2)) for start in range(2)],
+        tiled=True,
+    ).astype(jnp.float32)
 
     def temporal_back():
         grad_packed = local_call(

time: 242 us -> 227 us (0.938)
  waiting for transfers between devices: 37.4 us -> 24.1 us
  starting transfers between devices: 7.74 us -> 0.01 us
  Pallas kernels: 119 us -> 124 us
  local copies, waits for them, and re-layouts: 28 us -> 30.6 us
    unnamed x2, waiting for transfers between devices: 37.4 us -> 19.7 us
    ppermute x6 -> x1, starting transfers between devices: 7.71 us -> 0.01 us  [shards(): taken = lax.ppermute(given, 'dev', [(i, i ^ 1) for i in range(devices)])]
    concatenate x3 -> x0, other arithmetic: 7.2 us -> none  [neighbours(): return jnp.concatenate([before, array, after], axis=0)]
    ppermute x6 -> x1, waiting for transfers between devices: 0.02 us -> 4.34 us  [shards(): taken = lax.ppermute(given, 'dev', [(i, i ^ 1) for i in range(devices)])]
    slice x3 -> x0, local copies, waits for them, and re-layouts: 3.94 us -> none  [neighbours(): before = lax.ppermute(array[length - rows:], ('grp', 'dev'), up)]
    convert_element_type x1 -> x2, other arithmetic: 0.98 us -> 4.9 us  [the longest x1 3.93 us: shards(): (kept.astype(jnp.float32) + taken.astype(jnp.float32)).astype(jnp.bfloat16)]
    squeeze x0 -> x1, local copies, waits for them, and re-layouts: none -> 3 us  [shards(): given = lax.dynamic_index_in_dim(part, 1 - core, axis=1, keepdims=False)]
    pallas_call x1, Pallas kernels: 5.49 us -> 8.23 us  [spread(): pl.pallas_call(functools.partial(spread_kernel, count), out_shape=(jax.Sh...]
  transfers between devices with their start and end apart: 7 -> 2, of which waited for: 1 -> 2; matrix products, arithmetic and copies ran while one was open for 17% -> 0% of each run, Pallas kernels for 49% -> 51%
where the time goes in v1:
time: 227 us
  Pallas kernels  124 us (55%)
  local copies, waits for them, and re-layouts  30.6 us (13%)
  waiting for transfers between devices  24.1 us (11%)
  matrix products  22 us (10%)
  between operations  13.5 us (6%)
  other arithmetic  12.6 us (6%)
    pallas_call x1, Pallas kernels, collect(): pl.pallas_call(functools.partial(collect_kernel, count), out_shape=(jax.S...  115 us
    unnamed x2, waiting for transfers between devices  19.7 us
    dot_general x1, matrix products, spatial_forward(): jnp.dot(normed, in_proj, preferred_element_type=jnp.float32)  10.2 us
    reshape x1, local copies, waits for them, and re-layouts, spatial_forward(): packed = packed.reshape(frame_count, patches, 3, HEADS, HEAD_DIM)  9.86 us
    pallas_call x1, Pallas kernels, spread(): pl.pallas_call(functools.partial(spread_kernel, count), out_shape=(jax.Sh...  8.23 us
    another operation x8, local copies, waits for them, and re-layouts  7.28 us
    dot_general x1, matrix products, contract_rows(): lax.dot_general(left, right, (((0,), (0,)), ((), ())), preferred_element_...  5.68 us
  transfers between devices with their start and end apart: 2, of which 2 were waited for; matrix products, arithmetic and copies ran while one was open for 0% of the time, Pallas kernels for 51%

profile of v1, /device:TPU:0, one launch (start us, length us, event | category | flops | bytes accessed | tf_op | source)
XLA Modules:
  0.0 226.9 jit_solution(1151917109920101048)
XLA Ops:
  6.5 0.0 reduce-scatter.4.cloned.1.call-start
  6.6 0.0 copy-start.9
  6.6 0.0 copy-start
  6.6 41.4 %conditional.4 = (bf16[64,128]{1,0:T(8,128)(2,1)S(1)}, bf16[320,1408]{1,0:T(8,128)(2,1)}, bf16[384,1408]{1,0:T(8,128)(2,1)S(1)}, f32[64,128]{1,0:T(8,128)S(1)}) conditional(s32[]{:T(128)} %convert_element_type.105, (bf16[384,1408]{1,0:T(8,128)(2,1)}, bf16[1408,1408]{1,0:T(8,128)(2,1)}) %tuple.68, (bf16[5,64,1408]{2,1,0:T(8,128)(2,1)}, ...), branch_computations={%region_0.1_spmd, %region_1.7_spmd} | conditional | flops 3969696256 | bytes 47107628 | solution.py:514
  6.6 1.6 multiply_reduce_fusion.1
  8.2 0.1 rsqrt.22
  8.3 0.7 reduce.2
  9.0 1.4 fusion.9
  10.5 10.2 %convolution_convert_fusion.2 = bf16[320,4224]{1,0:T(8,128)(2,1)} fusion(bf16[320,1408]{1,0:T(8,128)(2,1)S(1)} %fusion.9, bf16[1408,4224]{1,0:T(8,128)(2,1)} %get-tuple-element.86), kind=kOutput, calls=%fused_computation.11 | convolution fusion | flops 3807682560 | bytes 15499264 | tf_op jit(solution)/shard_map/cond/branch_1_fun/dot_general | solution.py:478
  20.7 9.9 %reshape.149 = bf16[5,64,3,16,88]{4,3,2,1,0:T(8,128)(2,1)} reshape(bf16[320,4224]{1,0:T(8,128)(2,1)} %convolution_convert_fusion.2) | data formatting | bytes 5406720 | tf_op jit(solution)/shard_map/cond/branch_1_fun/reshape | solution.py:479
  30.5 3.0 %fusion.33 = (bf16[5,64,1,16,88]{4,3,2,1,0:T(8,128)(2,1)S(1)}, bf16[5,64,1,16,88]{4,3,2,1,0:T(8,128)(2,1)S(1)}, bf16[5,64,1,16,88]{4,3,2,1,0:T(8,128)(2,1)S(1)}) fusion(bf16[5,64,3,16,88]{4,3,2,1,0:T(8,128)(2,1)} %reshape.149), kind=kLoop, calls=%fused_computation.79 | loop fusion | bytes 5406720 | tf_op jit(solution)/shard_map/cond/branch_1_fun/slice | solution.py:491
  33.6 0.8 fusion.11
  34.4 3.9 %fusion.34 = (f32[5,16,64]{2,1,0:T(8,128)S(1)}, f32[5,16,64,64]{2,3,1,0:T(8,128)S(1)}) fusion(f32[5,16,64,64]{2,3,1,0:T(8,128)S(1)} %fusion.11), kind=kOutput, calls=%fused_computation.80 | output fusion | flops 1310783 | bytes 2641920 | tf_op jit(solution)/shard_map/cond/branch_1_fun/sub | solution.py:489
  38.3 2.0 convert_reduce_fusion
  40.3 0.1 reduce_sum.53
  40.4 2.8 %fusion.18 = f32[10,1408]{1,0:T(8,128)S(1)} fusion(bf16[1408,1408]{1,0:T(8,128)(2,1)} %get-tuple-element.87, bf16[5,1408]{1,0:T(8,128)(2,1)S(1)} %get-tuple-element.174, bf16[5,1408]{1,0:T(8,128)(2,1)S(1)} %get-tuple-element.173), kind=kOutput, calls=%fused_computation.37 | convolution fusion | flops 39705600 | bytes 4049408 | tf_op jit(solution)/shard_map/cond/branch_1_fun/dot_general | solution.py:497
  43.2 0.1 pad_reduce_fusion
  43.3 0.1 reshape.153
  43.5 2.2 copy.29
  45.6 2.2 reshape.152
  47.8 0.1 broadcast.180
  47.9 0.0 copy-start.6
  47.9 0.0 copy-start.7
  48.0 0.0 copy-start.8
  48.0 1.0 copy-done.6
  48.9 0.0 copy-done.9
  48.9 0.0 copy-done
  48.9 8.2 %shard_map.96 = (bf16[16,64,128]{2,1,0:T(8,128)(2,1)S(1)}, bf16[896,1408]{1,0:T(8,128)(2,1)}, bf16[640,1408]{1,0:T(8,128)(2,1)S(1)}, s32[7,8,128]{2,1,0:T(8,128)S(1)}) custom-call(bf16[64,128]{1,0:T(8,128)(2,1)S(1)} %get-tuple-element.133.own, bf16[384,1408]{1,0:T(8,128)(2,1)S(1)} %copy-done, bf16[384,1408]{1,0:T(8,128)(2,1)} %copy-done.6, ...), custom_call_target="tpu_custom_call" | custom-call | tf_op jit(solution)/shard_map/pallas_call | solution.py:177
  57.2 0.0 copy-done.7
  57.2 0.0 copy-done.8
  57.2 13.3 %conditional.5 = (bf16[896,4224]{1,0:T(8,128)(2,1)}, f32[640,128]{1,0:T(8,128)}, f32[640,128]{1,0:T(8,128)}, bf16[384,80]{1,0:T(8,128)(2,1)}, f32[384,1408]{1,0:...) conditional(s32[]{:T(128)} %convert_element_type.105, (bf16[896,1408]{1,0:T(8,128)(2,1)}, ...), branch_computations={%region_7.9_spmd, %region_9.10_spmd} | conditional | flops 12396882944 | bytes 58817752 | solution.py:551
  57.6 5.7 %convolution_convert_fusion.1 = bf16[1408,1408]{1,0:T(8,128)(2,1)} fusion(bf16[320,1408]{1,0:T(8,128)(2,1)} %get-tuple-element.100, bf16[320,1408]{1,0:T(8,128)(2,1)} %bitcast.99), kind=kOutput, calls=%fused_computation.2 | convolution fusion | flops 1270759424 | bytes 5767168 | tf_op jit(solution)/shard_map/cond/branch_1_fun/dot_general | solution.py:33
  63.3 3.5 %broadcast.185 = bf16[896,4224]{1,0:T(8,128)(2,1)} broadcast(bf16[]{:T(256)} %constant.71.clone), dimensions={} | broadcast | bytes 7569410 | tf_op jit(solution)/shard_map/broadcast.31
  66.8 1.5 broadcast.188
  68.3 0.7 broadcast.186
  69.0 0.8 broadcast.186.clone
  69.8 0.6 broadcast.187
  70.4 3.0 %dynamic-slice_bitcast_fusion = bf16[8,88,1408]{2,1,0:T(8,128)(2,1)} fusion(bf16[8,2,88,1408]{3,2,1,0:T(8,128)(2,1)} %get-tuple-element.140, s32[]{:T(128)S(6)} %select_n.36), kind=kLoop, calls=%fused_computation.72 | loop fusion | bytes 3964932 | tf_op jit(solution)/shard_map/jit(dynamic_index_in_dim)/squeeze | solution.py:557
  73.4 0.0 collective-permute-start
  73.5 4.3 %collective-permute-done = bf16[8,88,1408]{2,1,0:T(8,128)(2,1)} collective-permute-done((bf16[8,88,1408]{2,1,0:T(8,128)(2,1)}, bf16[8,88,1408]{2,1,0:T(8,128)(2,1)}, u32[]{:S(2)}, u32[]{:S(2)}) %collective-permute-start) | collective-permute-done | bytes 1982496 | tf_op jit(solution)/shard_map/ppermute | solution.py:558
  77.8 3.9 %fusion.31 = bf16[8,88,1408]{2,1,0:T(8,128)(2,1)} fusion(bf16[8,88,1408]{2,1,0:T(8,128)(2,1)} %collective-permute-done, bf16[8,2,88,1408]{3,2,1,0:T(8,128)(2,1)} %get-tuple-element.140, s32[]{:T(128)S(6)} %select_n.35), kind=kLoop, calls=%fused_computation.71 | loop fusion | flops 3964928 | bytes 5947396 | tf_op jit(solution)/shard_map/convert_element_type | solution.py:559
  81.7 0.0 reduce-scatter.4.cloned.1.call-update
  81.7 0.1 conditional.6
  81.8 115.3 %shard_map.97 = (bf16[16,64,128]{2,1,0:T(8,128)(2,1)S(1)}, f32[16,64,128]{2,1,0:T(8,128)S(1)}) custom-call(bf16[16,64,128]{2,1,0:T(8,128)(2,1)S(1)} %get-tuple-element.210.parts, f32[64,128]{1,0:T(8,128)S(1)} %get-tuple-element.147.sums), custom_call_target="tpu_custom_call" | custom-call | tf_op jit(solution)/shard_map/pallas_call | solution.py:298
  197.1 19.7 %reduce-scatter.4.cloned.1.call-done = bf16[88,1408]{1,0:T(8,128)(2,1)} async-done(((bf16[704,1408]{1,0:T(8,128)(2,1)}), bf16[88,1408]{1,0:T(8,128)(2,1)}) %reduce-scatter.4.cloned.1.call-update) | async-done | bytes 247824
  216.8 1.0 convert_element_type.110
  217.8 1.5 conditional.7
  217.8 0.3 copy.51
  218.2 0.1 reshape.162
  218.3 0.2 copy.52
  218.5 0.2 reshape.164
  218.7 0.6 fusion.1
  219.3 0.0 copy-start.5
  219.3 0.8 copy-done.5
  (11 shorter events, 0.2 us)
Async XLA Ops:
  6.5 210.3 %reduce-scatter.4.cloned.1.call-start = ((), (), s32[]{:S(2)}) async-start(), calls=%async_computation.1 | async-start | bytes 2230272
  6.6 42.4 %copy-start.9 = (s32[384]{0:T(512)S(1)}, s32[384]{0:T(512)}, u32[]{:S(2)}) copy-start(s32[384]{0:T(512)} %param.19) | copy-start | bytes 4612
  6.6 42.4 %copy-start = (bf16[384,1408]{1,0:T(8,128)(2,1)S(1)}, bf16[384,1408]{1,0:T(8,128)(2,1)}, u32[]{:S(2)}) copy-start(bf16[384,1408]{1,0:T(8,128)(2,1)} %tokens.1) | copy-start | bytes 3244036
  47.9 1.0 copy-start.6
  47.9 9.2 %copy-start.7 = (f32[1,1408]{1,0:T(1,128)S(1)}, f32[1,1408]{1,0:T(1,128)}, u32[]{:S(2)}) copy-start(f32[1,1408]{1,0:T(1,128)} %param.21) | copy-start | bytes 16900
  48.0 9.2 %copy-start.8 = (s32[80]{0:T(128)S(1)}, s32[80]{0:T(128)}, u32[]{:S(2)}) copy-start(s32[80]{0:T(128)} %param.18) | copy-start | bytes 964
  73.4 4.3 %collective-permute-start = (bf16[8,88,1408]{2,1,0:T(8,128)(2,1)}, bf16[8,88,1408]{2,1,0:T(8,128)(2,1)}, u32[]{:S(2)}, u32[]{:S(2)}) collective-permute-start(bf16[8,88,1408]{2,1,0:T(8,128)(2,1)} %dynamic-slice_bitcast_fusion), channel_id=1, source_target_pairs={{0,1},{1,0},{2,3},{3,2},{4,5},{5,4},{6,7},{7,6},{8,9},{9,8},{10,11... | collective-permute-start | bytes 5947400 | tf_op jit(solution)/shard_map/ppermute | solution.py:558
  219.3 0.8 copy-start.5
Sparse Core Ops, SparseCore 0:
  81.9 134.9 reduce-scatter.3

commit v2 on v1

--- a/solution.py
+++ b/solution.py
@@ -353,9 +353,8 @@
     ref[rows, columns] = jnp.where(mask, value, old).astype(ref.dtype)
 
 
-def attend_kernel(packed, grad, bias, mixed, log_total, row_delta):
+def attend_kernel(chosen, packed, grad, bias, log_total, row_delta, mixed=None):
     width = grad.shape[1]
-    blocks = grad.shape[0] // SPAN
     lanes = lax.broadcasted_iota(jnp.int32, (1, 128), 1)
 
     def one_head(head, carry):
@@ -364,7 +363,7 @@
         here = pl.ds(start, WINDOW)
         key_at = pl.ds(pl.multiple_of(start + width, 128), WINDOW)
         value_at = pl.ds(pl.multiple_of(start + 2 * width, 128), WINDOW)
-        for i in range(blocks):
+        for place, i in enumerate(chosen):
             query = packed[block(i + 1), here] * keep
             logits = dot_cols(query, packed[block(i, 3), key_at]) + bias[:, block(i, 3)]
             top = jnp.max(logits, axis=-1, keepdims=True)
@@ -377,10 +376,10 @@
             delta = jnp.sum(jnp.where(mask, product, 0.0), axis=-1, keepdims=True)
             own = lanes == head
             every = slice(0, 128)
-            blend(log_total, block(i), every, own, top * SCALE + jnp.log(total))
-            blend(row_delta, block(i), every, own, delta)
-            if 1 <= i < blocks - 1:
-                blend(mixed, block(i - 1), here, mask, value)
+            blend(log_total, block(place), every, own, top * SCALE + jnp.log(total))
+            blend(row_delta, block(place), every, own, delta)
+            if mixed is not None:
+                blend(mixed, block(place), here, mask, value)
         return carry
 
     lax.fori_loop(0, HEADS, one_head, 0, unroll=2)
@@ -527,10 +526,10 @@
         scaled_rows, inverse = normalize(inputs)
         normed = (scaled_rows * norm_gain).astype(jnp.bfloat16)
         packed = jnp.dot(normed, in_proj, preferred_element_type=jnp.float32).astype(jnp.bfloat16)
-        stat = jax.ShapeDtypeStruct(((blocks + 2) * SPAN, 128), jnp.float32)
-        time_mixed, log_total, row_delta = local_call(
-            attend_kernel,
-            (jax.ShapeDtypeStruct((token_count, width), jnp.bfloat16), stat, stat),
+        stat = jax.ShapeDtypeStruct((blocks * SPAN, 128), jnp.float32)
+        log_total, row_delta, time_mixed = local_call(
+            functools.partial(attend_kernel, range(1, blocks + 1)),
+            (stat, stat, jax.ShapeDtypeStruct((token_count, width), jnp.bfloat16)),
             packed, grad_mixed, bias,
         )
         part = contract_rows(time_mixed, time_cotangent).astype(jnp.bfloat16)
@@ -551,25 +550,23 @@
     part, packed, log_total, row_delta, selector, scaled_rows, inverse = lax.cond(
         spatial, from_frames, temporal_forward
     )
-    core = lax.rem(lax.axis_index("dev"), 2)
-    part = part.reshape(devices // 2, 2, width // devices, width)
-    kept = lax.dynamic_index_in_dim(part, core, axis=1, keepdims=False)
-    given = lax.dynamic_index_in_dim(part, 1 - core, axis=1, keepdims=False)
-    taken = lax.ppermute(given, "dev", [(i, i ^ 1) for i in range(devices)])
-    pair = (kept.astype(jnp.float32) + taken.astype(jnp.float32)).astype(jnp.bfloat16)
-    weight_part = lax.psum_scatter(
-        pair.reshape(width // 2, width),
-        "dev",
-        scatter_dimension=0,
-        axis_index_groups=[list(range(start, devices, 2)) for start in range(2)],
-        tiled=True,
-    ).astype(jnp.float32)
+    weight_part = lax.psum_scatter(part, "dev", scatter_dimension=0, tiled=True).astype(jnp.float32)
 
     def temporal_back():
+        stat = jax.ShapeDtypeStruct((2 * SPAN, 128), jnp.float32)
+        sides = local_call(
+            functools.partial(attend_kernel, (0, blocks + 1)),
+            (stat, stat),
+            packed, grad_mixed, bias,
+        )
+        stats = [
+            jnp.concatenate([side[:SPAN], own, side[SPAN:]], axis=0)
+            for side, own in zip(sides, (log_total, row_delta))
+        ]
         grad_packed = local_call(
             grads_kernel,
             jax.ShapeDtypeStruct((token_count, 3 * width), jnp.bfloat16),
-            packed, grad_mixed, bias, log_total, row_delta,
+            packed, grad_mixed, bias, *stats,
         )
         grad_scaled = contract_cols(grad_packed, in_proj) * norm_gain
         grad_inputs = inverse * (

time: 227 us -> 210 us (0.925)
  waiting for transfers between devices: 24.1 us -> 16.3 us
  local copies, waits for them, and re-layouts: 30.6 us -> 24.2 us
  other arithmetic: 12.6 us -> 8.71 us
    ppermute x1 -> x0, waiting for transfers between devices: 4.34 us -> none  [shards(): taken = lax.ppermute(given, 'dev', [(i, i ^ 1) for i in range(devices)])]
    convert_element_type x2 -> x1, other arithmetic: 4.9 us -> 0.98 us  [shards(): lax.psum_scatter(part, 'dev', scatter_dimension=0, tiled=True)]
    unnamed x2, waiting for transfers between devices: 19.7 us -> 16.3 us
    squeeze x1 -> x0, local copies, waits for them, and re-layouts: 3 us -> none  [shards(): given = lax.dynamic_index_in_dim(part, 1 - core, axis=1, keepdims=False)]
  transfers between devices with their start and end apart: 2 -> 1, of which waited for: 2 -> 1; matrix products, arithmetic and copies ran while one was open for 0% -> 0% of each run, Pallas kernels for 51% -> 55%
where the time goes in v2:
time: 210 us; the launch traced here: 209 us
  Pallas kernels  125 us (60%)
  local copies, waits for them, and re-layouts  24.2 us (12%)
  matrix products  21.1 us (10%)
  waiting for transfers between devices  16.3 us (8%)
  between operations  13.5 us (6%)
  other arithmetic  8.71 us (4%)
    pallas_call x1, Pallas kernels, collect(): pl.pallas_call(functools.partial(collect_kernel, count), out_shape=(jax.S...  116 us
    unnamed x2, waiting for transfers between devices  16.3 us
    dot_general x1, matrix products, spatial_forward(): jnp.dot(normed, in_proj, preferred_element_type=jnp.float32)  10.2 us
    reshape x1, local copies, waits for them, and re-layouts, spatial_forward(): packed = packed.reshape(frame_count, patches, 3, HEADS, HEAD_DIM)  9.86 us
    pallas_call x1, Pallas kernels, spread(): pl.pallas_call(functools.partial(spread_kernel, count), out_shape=(jax.Sh...  8.93 us
    another operation x8, local copies, waits for them, and re-layouts  6.17 us
    dot_general x1, matrix products, contract_rows(): lax.dot_general(left, right, (((0,), (0,)), ((), ())), preferred_element_...  5.82 us
  transfers between devices with their start and end apart: 1, of which 1 were waited for; matrix products, arithmetic and copies ran while one was open for 0% of the time, Pallas kernels for 55%

profile of v2, /device:TPU:0, one launch (start us, length us, event | category | flops | bytes accessed | tf_op | source)
XLA Modules:
  0.0 209.2 jit_solution(6588994228168837375)
XLA Ops:
  6.5 0.0 reduce-scatter.4.cloned.1.call-start
  6.6 0.0 copy-start.8
  6.6 0.0 copy-start
  6.6 40.0 %conditional.5 = (bf16[64,128]{1,0:T(8,128)(2,1)S(1)}, bf16[320,1408]{1,0:T(8,128)(2,1)}, bf16[384,1408]{1,0:T(8,128)(2,1)}, f32[64,128]{1,0:T(8,128)S(1)}) conditional(s32[]{:T(128)} %convert_element_type.92, (bf16[384,1408]{1,0:T(8,128)(2,1)}, bf16[1408,1408]{1,0:T(8,128)(2,1)}) %tuple.74, (bf16[5,64,1408]{2,1,0:T(8,128)(2,1)}, ...), branch_computations={%region_0.1_spmd, %region_1.7_spmd} | conditional | flops 3969696256 | bytes 47107628 | solution.py:513
  6.6 0.8 reduce.2
  7.4 1.5 multiply_reduce_fusion.1
  8.9 0.1 rsqrt.22
  9.0 1.4 fusion.9
  10.5 10.2 %convolution_convert_fusion.1 = bf16[320,4224]{1,0:T(8,128)(2,1)} fusion(bf16[320,1408]{1,0:T(8,128)(2,1)S(1)} %fusion.9, bf16[1408,4224]{1,0:T(8,128)(2,1)} %get-tuple-element.93), kind=kOutput, calls=%fused_computation.10 | convolution fusion | flops 3807682560 | bytes 15499264 | tf_op jit(solution)/shard_map/cond/branch_1_fun/dot_general | solution.py:477
  20.7 9.9 %reshape.140 = bf16[5,64,3,16,88]{4,3,2,1,0:T(8,128)(2,1)} reshape(bf16[320,4224]{1,0:T(8,128)(2,1)} %convolution_convert_fusion.1) | data formatting | bytes 5406720 | tf_op jit(solution)/shard_map/cond/branch_1_fun/reshape | solution.py:478
  30.5 3.0 %fusion.32 = (bf16[5,64,1,16,88]{4,3,2,1,0:T(8,128)(2,1)S(1)}, bf16[5,64,1,16,88]{4,3,2,1,0:T(8,128)(2,1)S(1)}, bf16[5,64,1,16,88]{4,3,2,1,0:T(8,128)(2,1)S(1)}) fusion(bf16[5,64,3,16,88]{4,3,2,1,0:T(8,128)(2,1)} %reshape.140), kind=kLoop, calls=%fused_computation.76 | loop fusion | bytes 5406720 | tf_op jit(solution)/shard_map/cond/branch_1_fun/slice | solution.py:490
  33.6 0.8 fusion.11
  34.4 3.9 %fusion.33 = (f32[5,16,64]{2,1,0:T(8,128)S(1)}, f32[5,16,64,64]{2,3,1,0:T(8,128)S(1)}) fusion(f32[5,16,64,64]{2,3,1,0:T(8,128)S(1)} %fusion.11), kind=kOutput, calls=%fused_computation.77 | output fusion | flops 1310783 | bytes 2641920 | tf_op jit(solution)/shard_map/cond/branch_1_fun/sub | solution.py:488
  38.3 0.9 convert_reduce_fusion
  39.2 0.9 copy.29
  40.1 2.2 %reshape.143 = bf16[320,1408]{1,0:T(8,128)(2,1)} reshape(bf16[5,64,16,88]{3,2,1,0:T(8,128)(2,1)S(1)} %copy.29) | data formatting | bytes 1802240 | tf_op jit(solution)/shard_map/cond/branch_1_fun/reshape | solution.py:492
  42.3 0.1 reshape.144
  42.5 0.1 reduce_sum.53
  42.6 2.8 %fusion.18 = f32[10,1408]{1,0:T(8,128)S(1)} fusion(bf16[1408,1408]{1,0:T(8,128)(2,1)} %get-tuple-element.94, bf16[5,1408]{1,0:T(8,128)(2,1)S(1)} %get-tuple-element.183, bf16[5,1408]{1,0:T(8,128)(2,1)S(1)} %get-tuple-element.182), kind=kOutput, calls=%fused_computation.36 | convolution fusion | flops 39705600 | bytes 4049408 | tf_op jit(solution)/shard_map/cond/branch_1_fun/dot_general | solution.py:496
  45.4 0.1 pad_reduce_fusion
  45.5 1.1 broadcast.178
  46.6 0.0 copy-start.3
  46.6 0.0 copy-start.6
  46.6 0.0 copy-start.7
  46.6 0.0 copy-done.8
  46.6 0.0 copy-done
  46.6 8.9 %shard_map.96 = (bf16[16,64,128]{2,1,0:T(8,128)(2,1)S(1)}, bf16[896,1408]{1,0:T(8,128)(2,1)}, bf16[640,1408]{1,0:T(8,128)(2,1)}, s32[7,8,128]{2,1,0:T(8,128)S(1)}) custom-call(bf16[64,128]{1,0:T(8,128)(2,1)S(1)} %get-tuple-element.142.own, bf16[384,1408]{1,0:T(8,128)(2,1)S(1)} %copy-done, bf16[384,1408]{1,0:T(8,128)(2,1)} %get-tuple-element.143.grads, ...), custom_call_target="tpu_custom_call" | custom-call | tf_op jit(solution)/shard_map/pallas_call | solution.py:177
  55.6 0.0 copy-done.3
  55.6 0.0 copy-done.6
  55.6 0.0 copy-done.7
  55.6 11.1 %conditional.6 = (bf16[1408,1408]{1,0:T(8,128)(2,1)}, bf16[896,4224]{1,0:T(8,128)(2,1)}, f32[384,128]{1,0:T(8,128)}, f32[384,128]{1,0:T(8,128)}, bf16[384,80]{1,...) conditional(s32[]{:T(128)} %convert_element_type.92, (bf16[896,1408]{1,0:T(8,128)(2,1)}, ...), branch_computations={%region_7.9_spmd, %region_9.10_spmd} | conditional | flops 12394900480 | bytes 61701336
  55.8 5.8 %fusion.36 = bf16[1408,1408]{1,0:T(8,128)(2,1)} fusion(bf16[320,1408]{1,0:T(8,128)(2,1)} %get-tuple-element.107, bf16[320,1408]{1,0:T(8,128)(2,1)} %bitcast.90), kind=kOutput, calls=%fused_computation.80 | convolution fusion | flops 1268776960 | bytes 5767168 | tf_op jit(solution)/shard_map/cond/branch_1_fun/dot_general | solution.py:33
  61.6 0.7 broadcast.184.clone
  62.3 0.7 broadcast.184
  63.0 0.1 broadcast.186
  63.2 3.5 %broadcast.183 = bf16[896,4224]{1,0:T(8,128)(2,1)} broadcast(bf16[]{:T(256)} %constant.59.clone), dimensions={} | broadcast | bytes 7569410 | tf_op jit(solution)/shard_map/broadcast.31
  66.7 0.0 reduce-scatter.4.cloned.1.call-update
  66.7 0.3 conditional.7
  67.0 115.8 %shard_map.97 = (bf16[16,64,128]{2,1,0:T(8,128)(2,1)S(1)}, f32[16,64,128]{2,1,0:T(8,128)S(1)}) custom-call(bf16[16,64,128]{2,1,0:T(8,128)(2,1)S(1)} %get-tuple-element.225.parts, f32[64,128]{1,0:T(8,128)S(1)} %get-tuple-element.156.sums), custom_call_target="tpu_custom_call" | custom-call | tf_op jit(solution)/shard_map/pallas_call | solution.py:298
  182.8 16.3 %reduce-scatter.4.cloned.1.call-done = bf16[88,1408]{1,0:T(8,128)(2,1)} async-done(((bf16[1408,1408]{1,0:T(8,128)(2,1)}), bf16[88,1408]{1,0:T(8,128)(2,1)}) %reduce-scatter.4.cloned.1.call-update) | async-done | bytes 247824
  199.1 1.0 convert_element_type.94
  200.1 1.5 conditional.8
  200.1 0.3 copy.51
  200.4 0.1 reshape.151
  200.6 0.2 copy.52
  200.8 0.2 reshape.153
  201.0 0.6 fusion.1
  201.6 0.0 copy-start.4
  201.6 0.8 copy-done.4
  (12 shorter events, 0.2 us)
Async XLA Ops:
  6.5 192.5 %reduce-scatter.4.cloned.1.call-start = ((), (), s32[]{:S(2)}) async-start(), calls=%async_computation.1 | async-start | bytes 4212736
  6.6 40.0 %copy-start.8 = (s32[384]{0:T(512)S(1)}, s32[384]{0:T(512)}, u32[]{:S(2)}) copy-start(s32[384]{0:T(512)} %param.19) | copy-start | bytes 4612
  6.6 40.0 %copy-start = (bf16[384,1408]{1,0:T(8,128)(2,1)S(1)}, bf16[384,1408]{1,0:T(8,128)(2,1)}, u32[]{:S(2)}) copy-start(bf16[384,1408]{1,0:T(8,128)(2,1)} %tokens.1) | copy-start | bytes 3244036
  46.6 9.0 %copy-start.3 = (bf16[384,1408]{1,0:T(8,128)(2,1)S(1)}, bf16[384,1408]{1,0:T(8,128)(2,1)}, u32[]{:S(2)}) copy-start(bf16[384,1408]{1,0:T(8,128)(2,1)} %param.25) | copy-start | bytes 3244036
  46.6 9.0 %copy-start.6 = (f32[1,1408]{1,0:T(1,128)S(1)}, f32[1,1408]{1,0:T(1,128)}, u32[]{:S(2)}) copy-start(f32[1,1408]{1,0:T(1,128)} %param.21) | copy-start | bytes 16900
  46.6 9.0 %copy-start.7 = (s32[80]{0:T(128)S(1)}, s32[80]{0:T(128)}, u32[]{:S(2)}) copy-start(s32[80]{0:T(128)} %param.18) | copy-start | bytes 964
  201.6 0.8 copy-start.4
Sparse Core Ops, SparseCore 0:
  66.8 132.2 reduce-scatter.3
